TPU v7x, 512 devices: a whole 4x8x8 slice. The times are simulated.
512 devices in a mesh: clus: 32 (over y, x_lo, core), head: 16 (over z, x_hi).
Axes of the slice: x: 4 (x_hi: 2, x_lo: 2; x = x_hi * 2 + x_lo), y: 8, z: 8, core: 2. Of those that a mesh axis runs over, the one named last changes fastest.
Arguments:
- node_queries: bfloat16 [131072, 1024], P(('clus', 'head')), may hold values from -8 to 8
- node_keys: bfloat16 [131072, 1024], P(('clus', 'head')), may hold values from -8 to 8
- node_values: bfloat16 [131072, 1024], P(('clus', 'head')), may hold values from -6 to 6
- matchings: int32 [3, 32], replicated, may hold values from 0 to 31, as said below
- patterns: int32 [32, 32, 12], P('clus'), may hold values from 0 to 127, as said below
- out_gain: float32 [1024], replicated, may hold values from 0.5 to 1.5
Outputs:
- attended: bfloat16 [131072, 1024], P(('clus', 'head'))
Inputs may be any that keep to these rules, and one draw needn't show every extreme that they name: Each row is a perfect matching: matchings[j, c] != c and matchings[j, matchings[j, c]] == c. `patterns`: for every cluster and query block, entries s * 3 to (s + 1) * 3 - 1 are 3 different blocks of source s, that is numbers from s * 32 to (s + 1) * 32 - 1.
All inputs are finite; a program needn't handle non-finite values.
Results may differ from a plain program's by a relative error of at most 0.0057.
Values may be sent and summed in bfloat16 or wider, within the bound.
A program may use at most 64 MiB of HBM per device.

v0:
```python
import math

import jax
import jax.numpy as jnp
from jax import lax
from jax.sharding import PartitionSpec as P

HEAD_DIM = 64


group_blocks = 4


def attend_cluster(head_queries, key_rows, value_rows, pattern):
    row_count = head_queries.shape[0]
    feature_width = head_queries.shape[1]
    head_count = feature_width // HEAD_DIM
    block_rows = row_count // pattern.shape[0]
    groups = pattern.shape[0] // group_blocks
    score_scale = 1.0 / math.sqrt(HEAD_DIM)
    query_groups = head_queries.reshape(groups, group_blocks, block_rows, head_count, HEAD_DIM)
    key_blocks = key_rows.reshape(-1, block_rows, head_count, HEAD_DIM)
    value_blocks = value_rows.reshape(-1, block_rows, head_count, HEAD_DIM)
    pattern_groups = pattern.reshape(groups, group_blocks, -1)

    def one_group(inputs):
        query_group, chosen = inputs
        key_group = jnp.take(key_blocks, chosen, axis=0).reshape(
            group_blocks, -1, head_count, HEAD_DIM
        )
        value_group = jnp.take(value_blocks, chosen, axis=0).reshape(
            group_blocks, -1, head_count, HEAD_DIM
        )
        scores = (
            jnp.einsum(
                "bqhd,bkhd->bhqk", query_group, key_group, preferred_element_type=jnp.float32
            )
            * score_scale
        )
        maximum = jnp.max(scores, axis=-1, keepdims=True)
        powers = jnp.exp(scores - maximum)
        weights = (powers / jnp.sum(powers, axis=-1, keepdims=True)).astype(jnp.bfloat16)
        mixed_rows = jnp.einsum(
            "bhqk,bkhd->bqhd", weights, value_group, preferred_element_type=jnp.float32
        )
        return mixed_rows.astype(jnp.bfloat16)

    mixed_rows = lax.map(one_group, (query_groups, pattern_groups))
    return mixed_rows.reshape(row_count, feature_width)


def local(node_queries, node_keys, node_values, matchings, patterns, out_gain):
    head_queries, own_keys, own_values = (
        lax.all_to_all(node_queries, "head", split_axis=1, concat_axis=0, tiled=True),
        lax.all_to_all(node_keys, "head", split_axis=1, concat_axis=0, tiled=True),
        lax.all_to_all(node_values, "head", split_axis=1, concat_axis=0, tiled=True),
    )
    key_value = jnp.stack([own_keys, own_values])[None]
    spread = lax.all_to_all(key_value, "clus", split_axis=2, concat_axis=0, tiled=True)
    chosen = jnp.take(spread, matchings, axis=0)
    partner = lax.all_to_all(chosen, "clus", split_axis=1, concat_axis=3, tiled=True)
    partner_pairs = partner[:, 0]
    head_width = head_queries.shape[1]
    key_rows = jnp.concatenate([own_keys[None], partner_pairs[:, 0]], axis=0).reshape(
        -1, head_width
    )
    value_rows = jnp.concatenate([own_values[None], partner_pairs[:, 1]], axis=0).reshape(
        -1, head_width
    )
    mixed_rows = attend_cluster(head_queries, key_rows, value_rows, patterns[0])
    restored = lax.all_to_all(mixed_rows, "head", split_axis=0, concat_axis=1, tiled=True).astype(
        jnp.float32
    )
    mean_square = jnp.mean(restored * restored, axis=-1, keepdims=True)
    return (restored * lax.rsqrt(mean_square + 1e-06) * out_gain).astype(jnp.bfloat16)


def solution(mesh):
    in_specs = (
        P(("clus", "head"), None),
        P(("clus", "head"), None),
        P(("clus", "head"), None),
        P(),
        P("clus", None, None),
        P(),
    )
    out_specs = P(("clus", "head"), None)
    return jax.shard_map(local, mesh=mesh, in_specs=in_specs, out_specs=out_specs, check_vma=False)
```

profile of v0, /device:TPU:1, one launch (start us, length us, event | category | flops | bytes accessed | tf_op | source)
XLA Modules:
  0.0 377.4 jit_solution(7026153946690142072)
XLA Ops:
  0.0 2.1 copy.70
  2.1 13.4 %all-to-all-start.1 = ((bf16[256,16,64]{0,2,1:T(8,128)(2,1)}), bf16[256,16,64]{0,2,1:T(8,128)(2,1)S(1)}, u32[]{:S(2)}, u32[]{:S(2)}) async-start(bf16[256,16,64]{0,2,1:T(8,128)(2,1)} %bitcast.12), calls=%async_computation.1 | async-start | bytes 1048576 | tf_op jit(solution)/shard_map/all_to_all | solution.py:55
  16.6 16.1 %all-to-all-done.1 = bf16[256,16,64]{0,2,1:T(8,128)(2,1)S(1)} async-done(((bf16[256,16,64]{0,2,1:T(8,128)(2,1)}), bf16[256,16,64]{0,2,1:T(8,128)(2,1)S(1)}, u32[]{:S(2)}, u32[]{:S(2)}) %all-to-all-start.1) | async-done | bytes 524320 | tf_op jit(solution)/shard_map/all_to_all | solution.py:55
  32.7 4.8 %all-to-all-start = ((bf16[256,16,64]{0,2,1:T(8,128)(2,1)}), bf16[256,16,64]{0,2,1:T(8,128)(2,1)S(1)}, u32[]{:S(2)}, u32[]{:S(2)}) async-start(bf16[256,16,64]{0,2,1:T(8,128)(2,1)} %bitcast.10), calls=%async_computation | async-start | bytes 1048576 | tf_op jit(solution)/shard_map/all_to_all | solution.py:56
  38.0 16.6 %all-to-all-done = bf16[256,16,64]{0,2,1:T(8,128)(2,1)S(1)} async-done(((bf16[256,16,64]{0,2,1:T(8,128)(2,1)}), bf16[256,16,64]{0,2,1:T(8,128)(2,1)S(1)}, u32[]{:S(2)}, u32[]{:S(2)}) %all-to-all-start) | async-done | bytes 524320 | tf_op jit(solution)/shard_map/all_to_all | solution.py:56
  56.1 2.8 copy.72
  59.0 2.3 reshape.132
  61.2 9.9 %all-to-all-start.2 = ((bf16[32,2,8192]{2,1,0:T(2,128)(2,1)}), bf16[32,2,8192]{2,1,0:T(2,128)(2,1)S(1)}, u32[]{:S(2)}, u32[]{:S(2)}) async-start(bf16[32,2,8192]{2,1,0:T(2,128)(2,1)} %reshape.132), calls=%async_computation.2 | async-start | bytes 2097152 | tf_op jit(solution)/shard_map/all_to_all | solution.py:59
  72.1 27.1 %all-to-all-done.2 = bf16[32,2,8192]{2,1,0:T(2,128)(2,1)S(1)} async-done(((bf16[32,2,8192]{2,1,0:T(2,128)(2,1)}), bf16[32,2,8192]{2,1,0:T(2,128)(2,1)S(1)}, u32[]{:S(2)}, u32[]{:S(2)}) %all-to-all-start.2) | async-done | bytes 1048608 | tf_op jit(solution)/shard_map/all_to_all | solution.py:59
  99.2 4.2 %all-to-all-start.4 = ((bf16[256,16,64]{0,2,1:T(8,128)(2,1)}), bf16[256,16,64]{0,2,1:T(8,128)(2,1)}, u32[]{:S(2)}, u32[]{:S(2)}) async-start(bf16[256,16,64]{0,2,1:T(8,128)(2,1)} %bitcast.22), calls=%async_computation.4 | async-start | bytes 1048576 | tf_op jit(solution)/shard_map/all_to_all | solution.py:54
  105.1 3.0 copy.74
  108.1 2.7 gather_fusion.2
  110.9 3.9 %copy_select_fusion.2 = bf16[3,32,2,128,64]{3,4,2,0,1:T(8,128)(2,1)} fusion(bf16[3,32,2,128,64]{3,4,2,1,0:T(8,128)(2,1)} %bitcast.105, pred[3,32]{0,1:T(8,128)(4,1)S(1)} %copy.69), kind=kLoop, calls=%fused_computation.23 | loop fusion | flops 1572864 | bytes 6291552 | tf_op jit(solution)/shard_map/jit(_take)/select_n | solution.py:60
  114.8 6.0 %all-to-all-done.4 = bf16[256,16,64]{0,2,1:T(8,128)(2,1)} async-done(((bf16[256,16,64]{0,2,1:T(8,128)(2,1)}), bf16[256,16,64]{0,2,1:T(8,128)(2,1)}, u32[]{:S(2)}, u32[]{:S(2)}) %all-to-all-start.4) | async-done | bytes 524320 | tf_op jit(solution)/shard_map/all_to_all | solution.py:54
  120.7 6.9 %all-to-all-start.3 = ((bf16[3,32,2,128,64]{3,4,2,0,1:T(8,128)(2,1)}), bf16[3,32,2,128,64]{3,4,2,0,1:T(8,128)(2,1)S(1)}, u32[]{:S(2)}, u32[]{:S(2)}) async-start(bf16[3,32,2,128,64]{3,4,2,0,1:T(8,128)(2,1)} %copy_select_fusion.2), calls=%async_computation.3 | async-start | bytes 6291456 | tf_op jit(solution)/shard_map/all_to_all | solution.py:61
  127.7 2.1 copy.79
  129.9 2.0 reshape.84
  131.8 67.7 %all-to-all-done.3 = bf16[3,32,2,128,64]{3,4,2,0,1:T(8,128)(2,1)S(1)} async-done(((bf16[3,32,2,128,64]{3,4,2,0,1:T(8,128)(2,1)}), bf16[3,32,2,128,64]{3,4,2,0,1:T(8,128)(2,1)S(1)}, u32[]{:S(2)}, u32[]{:S(2)}) %all-to-all-start.3) | async-done | bytes 3145760 | tf_op jit(solution)/shard_map/all_to_all | solution.py:61
  199.5 3.7 copy.76
  203.2 4.1 %squeeze.15 = bf16[3,2,4096,64]{2,3,1,0:T(8,128)(2,1)S(1)} reshape(bf16[3,1,2,32,128,64]{4,3,5,2,0,1:T(8,128)(2,1)} %copy.76) | data formatting | bytes 6291456 | tf_op jit(solution)/shard_map/squeeze | solution.py:62
  208.5 1.7 pad_maximum_fusion
  211.9 3.3 reshape_reshape.6
  215.1 4.4 %copy.81 = bf16[128,128,1,64]{1,3,2,0:T(8,128)(2,1)} copy(bf16[128,128,1,64]{1,0,3,2:T(8,128)(2,1)} %reshape_reshape.6) | data formatting | bytes 4194304 | tf_op jit(solution)/shard_map/while | solution.py:48
  221.2 3.3 reshape_reshape.7
  224.5 3.0 copy.83
  227.5 130.3 %while.10 = (s32[]{:T(128)}, bf16[8,4,128,1,64]{2,1,0,4,3:T(4,128)(2,1)S(1)}, s32[8,4,12]{2,1,0:T(4,128)S(1)}, bf16[128,128,1,64]{1,3,2,0:T(8,128)(2,1)}, bf16[8...) while((s32[]{:T(128)}, bf16[8,4,128,1,64]{2,1,0,4,3:T(4,128)(2,1)S(1)}, ...), condition=%wide.region_3.5_spmd, body=%wide.region_0.4_spmd.sunk | while | flops 308319008 | bytes 29042224 | solution.py:48
  229.0 2.3 gather_fusion
  231.3 2.3 gather_fusion.1
  233.6 2.0 copy_select_fusion.4
  241.3 2.6 fusion.26
  245.3 2.3 gather_fusion
  247.6 2.3 gather_fusion.1
  249.9 2.0 copy_select_fusion.4
  257.5 2.6 fusion.26
  261.5 2.3 gather_fusion
  263.8 2.3 gather_fusion.1
  266.1 2.0 copy_select_fusion.4
  270.7 1.7 fusion.25
  273.8 2.6 fusion.26
  277.8 2.3 gather_fusion
  280.1 2.3 gather_fusion.1
  282.4 2.0 copy_select_fusion.4
  286.9 1.7 fusion.25
  290.0 2.6 fusion.26
  294.1 2.3 gather_fusion
  296.4 2.3 gather_fusion.1
  298.7 2.0 copy_select_fusion.4
  303.2 1.7 fusion.25
  306.3 2.6 fusion.26
  310.3 2.3 gather_fusion
  312.6 2.3 gather_fusion.1
  314.9 2.0 copy_select_fusion.4
  319.5 1.7 fusion.25
  322.6 2.6 fusion.26
  326.6 2.3 gather_fusion
  328.9 2.3 gather_fusion.1
  331.2 2.0 copy_select_fusion.4
  335.7 1.7 fusion.25
  338.8 2.6 fusion.26
  342.9 2.3 gather_fusion
  345.1 2.3 gather_fusion.1
  347.4 2.0 copy_select_fusion.4
  355.1 2.6 fusion.26
  358.3 17.7 %all_to_all.94 = bf16[16,256,64]{1,2,0:T(8,128)(2,1)S(1)} all-to-all(bf16[16,256,64]{1,2,0:T(8,128)(2,1)S(1)} %copy.85), channel_id=1, replica_groups=mesh['clus'=32,'head'=16] {'head'}, dimensions={0} | all-to-all | bytes 1048576 | tf_op jit(solution)/shard_map/all_to_all | solution.py:71
  (137 shorter events, 59.7 us)
Async XLA Ops:
  0.0 15.5 %copy-start.7 = (bf16[256,1024]{1,0:T(8,128)(2,1)S(1)}, bf16[256,1024]{1,0:T(8,128)(2,1)}, u32[]{:S(2)}) copy-start(bf16[256,1024]{1,0:T(8,128)(2,1)} %param.12) | copy-start | bytes 1572868
  2.1 30.6 %all-to-all-start.1 = ((bf16[256,16,64]{0,2,1:T(8,128)(2,1)}), bf16[256,16,64]{0,2,1:T(8,128)(2,1)S(1)}, u32[]{:S(2)}, u32[]{:S(2)}) async-start(bf16[256,16,64]{0,2,1:T(8,128)(2,1)} %bitcast.12), calls=%async_computation.1 | async-start | bytes 1048576 | tf_op jit(solution)/shard_map/all_to_all | solution.py:55
  32.7 22.0 %all-to-all-start = ((bf16[256,16,64]{0,2,1:T(8,128)(2,1)}), bf16[256,16,64]{0,2,1:T(8,128)(2,1)S(1)}, u32[]{:S(2)}, u32[]{:S(2)}) async-start(bf16[256,16,64]{0,2,1:T(8,128)(2,1)} %bitcast.10), calls=%async_computation | async-start | bytes 1048576 | tf_op jit(solution)/shard_map/all_to_all | solution.py:56
  38.0 17.2 %copy-start.3 = (bf16[1,4096,64]{1,2,0:T(8,128)(2,1)}, bf16[1,4096,64]{1,2,0:T(8,128)(2,1)S(1)}, u32[]{:S(2)}) copy-start(bf16[1,4096,64]{1,2,0:T(8,128)(2,1)S(1)} %broadcast_in_dim.41) | copy-start | bytes 1572868
  55.2 0.8 copy-start.5
  59.0 12.1 %copy-start.8 = (bf16[256,1024]{1,0:T(8,128)(2,1)S(1)}, bf16[256,1024]{1,0:T(8,128)(2,1)}, u32[]{:S(2)}) copy-start(bf16[256,1024]{1,0:T(8,128)(2,1)} %param.10) | copy-start | bytes 1572868
  61.2 42.3 %copy-start.10 = (s32[3,32]{1,0:T(4,128)S(1)}, s32[3,32]{1,0:T(4,128)}, u32[]{:S(2)}) copy-start(s32[3,32]{1,0:T(4,128)} %param.13) | copy-start | bytes 1156
  61.2 38.0 %all-to-all-start.2 = ((bf16[32,2,8192]{2,1,0:T(2,128)(2,1)}), bf16[32,2,8192]{2,1,0:T(2,128)(2,1)S(1)}, u32[]{:S(2)}, u32[]{:S(2)}) async-start(bf16[32,2,8192]{2,1,0:T(2,128)(2,1)} %reshape.132), calls=%async_computation.2 | async-start | bytes 2097152 | tf_op jit(solution)/shard_map/all_to_all | solution.py:59
  99.2 21.5 %all-to-all-start.4 = ((bf16[256,16,64]{0,2,1:T(8,128)(2,1)}), bf16[256,16,64]{0,2,1:T(8,128)(2,1)}, u32[]{:S(2)}, u32[]{:S(2)}) async-start(bf16[256,16,64]{0,2,1:T(8,128)(2,1)} %bitcast.22), calls=%async_computation.4 | async-start | bytes 1048576 | tf_op jit(solution)/shard_map/all_to_all | solution.py:54
  114.8 12.9 %copy-start.11 = (s32[1,32,12]{1,0,2:T(1,128)S(1)}, s32[1,32,12]{1,0,2:T(1,128)}, u32[]{:S(2)}) copy-start(s32[1,32,12]{1,0,2:T(1,128)} %param.14) | copy-start | bytes 4612
  120.7 78.8 %all-to-all-start.3 = ((bf16[3,32,2,128,64]{3,4,2,0,1:T(8,128)(2,1)}), bf16[3,32,2,128,64]{3,4,2,0,1:T(8,128)(2,1)S(1)}, u32[]{:S(2)}, u32[]{:S(2)}) async-start(bf16[3,32,2,128,64]{3,4,2,0,1:T(8,128)(2,1)} %copy_select_fusion.2), calls=%async_computation.3 | async-start | bytes 6291456 | tf_op jit(solution)/shard_map/all_to_all | solution.py:61
  207.3 1.0 copy-start.4
  207.3 1.2 copy-start.6
  215.1 4.4 %copy-start.2 = (bf16[4,4096,64]{1,2,0:T(8,128)(2,1)S(1)}, bf16[4,4096,64]{1,2,0:T(8,128)(2,1)}, u32[]{:S(2)}) copy-start(bf16[4,4096,64]{1,2,0:T(8,128)(2,1)} %get-tuple-element.82) | copy-start | bytes 6291460
  224.5 3.0 copy-start.9
  227.7 1.3 copy-start
  241.3 2.7 copy-start.1
  244.0 1.3 copy-start
  257.5 2.7 copy-start.1
  260.2 1.3 copy-start
  273.8 2.7 copy-start.1
  276.5 1.3 copy-start
  290.0 2.7 copy-start.1
  292.7 1.3 copy-start
  306.3 2.7 copy-start.1
  309.0 1.3 copy-start
  322.6 2.7 copy-start.1
  325.3 1.3 copy-start
  338.8 2.7 copy-start.1
  341.5 1.3 copy-start
  355.1 2.7 copy-start.1
  357.8 18.4 %copy-start.12 = (f32[1024]{0:T(1024)S(1)}, f32[1024]{0:T(1024)}, u32[]{:S(2)}) copy-start(f32[1024]{0:T(1024)} %param.15) | copy-start | bytes 12292
where the time goes:
time: 384 us; the launch traced here: 377 us
  waiting for transfers between devices  134 us (35%)
  local copies, waits for them, and re-layouts  129 us (34%)
  starting transfers between devices  39.2 us (10%)
  matrix products  34.1 us (9%)
  other arithmetic  22.3 us (6%)
  blocking collectives  17.7 us (5%)
    all_to_all x1, waiting for transfers between devices, local(): lax.all_to_all(chosen, 'clus', split_axis=1, concat_axis=3, tiled=True)  67.7 us
    all_to_all x1, waiting for transfers between devices, local(): lax.all_to_all(key_value, 'clus', split_axis=2, concat_axis=0, tiled=True)  27.1 us
    another operation x16, local copies, waits for them, and re-layouts  24.6 us
    dot_general x8, matrix products, one_group(): jnp.einsum('bhqk,bkhd->bqhd', weights, value_group, preferred_element_typ...  20.6 us
    gather x8, local copies, waits for them, and re-layouts, one_group(): jnp.take(value_blocks, chosen, axis=0)  18.3 us
    gather x8, local copies, waits for them, and re-layouts, one_group(): jnp.take(key_blocks, chosen, axis=0)  18.3 us
    all_to_all x1, blocking collectives, local(): lax.all_to_all(mixed_rows, 'head', split_axis=0, concat_axis=1, tiled=True)  17.7 us
    all_to_all x1, waiting for transfers between devices, local(): lax.all_to_all(node_values, 'head', split_axis=1, concat_axis=0, tiled=True)  16.6 us
  transfers between devices with their start and end apart: 5, of which 5 were waited for; matrix products, arithmetic and copies ran while one was open for 5% of the time, Pallas kernels for 0%

commit v1 on v0

v1 whole, which is shorter than its diff:
```python
import functools
import math

import jax
import jax.numpy as jnp
from jax import lax
from jax.experimental import pallas as pl
from jax.experimental.pallas import tpu as pltpu
from jax.sharding import PartitionSpec as P

HEAD_DIM = 64
BLOCK = 128
LANES = 128
PARTS = 2
ROWS = BLOCK // PARTS
PHASES = 2 * PARTS
NEAR = 4
MESH = pl.DeviceIdType.MESH


def attention_kernel(
    dims,
    tile_ref,
    half_ref,
    match_ref,
    q_ref,
    k_ref,
    v_ref,
    gain_ref,
    out_ref,
    packed,
    packed_q,
    staged,
    queries,
    powers,
    scores,
    masks,
    mixed_out,
    mixed_in,
    *rest,
):
    heads, ring, near, chosen = dims
    gathered = rest[:PHASES]
    selected = rest[PHASES : 2 * PHASES]
    (
        first_send,
        first_send_same,
        first_recv,
        ring_send,
        ring_recv,
        own_send,
        own_recv,
        partner_send,
        partner_recv,
        q_send,
        q_recv,
        mixed_send,
        mixed_recv,
    ) = rest[2 * PHASES :]
    tiles = heads // near
    sources = 4
    far = ring // 2
    sub = near // 2
    clus = lax.axis_index("clus")
    h = lax.axis_index("head")
    y = clus // near
    u = clus % near
    home = h % near
    same = home == u

    def copy(src, dst, send, recv, to_clus, to_head):
        return pltpu.make_async_remote_copy(
            src_ref=src,
            dst_ref=dst,
            send_sem=send,
            recv_sem=recv,
            device_id={"clus": to_clus, "head": to_head},
            device_id_type=MESH,
        )

    def arrived(ref, sem):
        pltpu.make_async_copy(ref, ref, sem).wait()

    barrier = pltpu.get_barrier_semaphore()

    def greet(to_clus, to_head):
        pl.semaphore_signal(
            barrier, inc=1, device_id={"clus": to_clus, "head": to_head}, device_id_type=MESH
        )

    def greet_first(i, carry):
        to_clus = y * near + i // tiles
        to_head = u + near * (i % tiles)

        @pl.when(jnp.logical_or(to_clus != clus, to_head != h))
        def _():
            greet(to_clus, to_head)

        return carry

    def greet_head(r, carry):
        greet(clus, (h + r) % heads)
        return carry

    lax.fori_loop(0, near * tiles, greet_first, 0)
    lax.fori_loop(1, heads, greet_head, 0)
    for r in range(1, near):
        greet(y * near + (u + r) % near, h)
    above = ((y + 1) % ring) * near + u
    below = ((y + ring - 1) % ring) * near + u
    greet(above, h)
    greet(below, h)

    def pack(ref, put):
        for t in range(heads // 2):
            first = ref[0:BLOCK, t * LANES : (t + 1) * LANES]
            second = ref[BLOCK : 2 * BLOCK, t * LANES : (t + 1) * LANES]
            put(
                2 * t,
                jnp.concatenate([first[:, :HEAD_DIM], second[:, :HEAD_DIM]], axis=1),
            )
            put(
                2 * t + 1,
                jnp.concatenate([first[:, HEAD_DIM:], second[:, HEAD_DIM:]], axis=1),
            )

    def put_rows(which):
        def put(head, tile):
            for part in range(PARTS):
                packed[which * PARTS + part, head] = tile[part * ROWS : (part + 1) * ROWS]

        return put

    def put_q(head, tile):
        packed_q[head] = tile

    pack(k_ref, put_rows(0))
    lane = lax.broadcasted_iota(jnp.int32, (16, LANES), 1)
    masks[0] = jnp.where(lane < HEAD_DIM, 1.0, 0.0).astype(masks.dtype)
    masks[1] = jnp.where(lane < HEAD_DIM, 0.0, 1.0).astype(masks.dtype)

    itself = jnp.where(same, 1, 0)
    pl.semaphore_wait(barrier, (near * tiles - itself) + (heads - 1) + (near - 1) + 2)

    def first_copy(p, r):
        g = (h + r) % heads
        return copy(
            packed.at[p, g],
            gathered[p].at[clus, h // near],
            first_send.at[p],
            first_recv.at[p],
            y * near + home,
            g,
        )

    def first_copy_same(p):
        return copy(
            packed.at[p, h],
            gathered[p].at[clus, h // near],
            first_send_same.at[p],
            first_recv.at[p],
            y * near + home,
            h,
        )

    def first_start(p):
        @pl.when(same)
        def _():
            pltpu.make_async_copy(
                packed.at[p, h], gathered[p].at[clus, h // near], first_recv.at[p]
            ).start()

        @pl.when(jnp.logical_not(same))
        def _():
            first_copy_same(p).start()

        def step(r, carry):
            first_copy(p, r).start()
            return carry

        lax.fori_loop(1, heads, step, 0)

    def q_start():
        pltpu.make_async_copy(packed_q.at[h], queries.at[h], q_recv).start()

        def step(r, carry):
            g = (h + r) % heads
            copy(packed_q.at[g], queries.at[h], q_send, q_recv, clus, g).start()
            return carry

        lax.fori_loop(1, heads, step, 0)

    def ring_copy(p, way, step, part):
        if way == 0:
            slot, to = (y + ring - (step - 1)) % ring, above
        else:
            slot, to = (y + step - 1) % ring, below
        ref = gathered[p].at[pl.ds(slot * near + part * sub, sub)]
        return copy(
            ref,
            ref,
            ring_send.at[p, way, step - 1, part],
            ring_recv.at[p, way, step - 1, part],
            to,
            h,
        )

    def ring_wait(p, way, step, part):
        slot = (y + ring - step) % ring if way == 0 else (y + step) % ring
        arrived(
            gathered[p].at[pl.ds(slot * near + part * sub, sub)],
            ring_recv.at[p, way, step - 1, part],
        )

    def own_copy(p, r):
        to = y * near + (u + r) % near
        return copy(
            gathered[p].at[to],
            selected[p].at[pl.ds(u * sources * tiles, tiles)],
            own_send.at[p, r - 1],
            own_recv.at[p, r - 1],
            to,
            h,
        )

    def partner_copy(p, r):
        return copy(
            staged.at[p, r - 1],
            selected[p].at[pl.ds((u * sources + 1) * tiles, (sources - 1) * tiles)],
            partner_send.at[p, r - 1],
            partner_recv.at[p, r - 1],
            y * near + (u + r) % near,
            h,
        )

    def enter(p):
        arrived(gathered[p].at[pl.ds(y * near, near)], first_recv.at[p])
        for part in range(2):
            for way in range(2):
                ring_copy(p, way, 1, part).start()
        for r in range(1, near):
            own_copy(p, r).start()

    def forward(p, step, between=lambda: None):
        for part in range(2):
            for way in range(2):
                ring_wait(p, way, step - 1, part)
                if step < far or part == way:
                    ring_copy(p, way, step, part).start()
            between()

    def leave(p):
        for way in range(2):
            ring_wait(p, way, far, way)
        for r in range(1, near):
            to = y * near + (u + r) % near
            for j in range(sources - 1):
                staged[p, r - 1, j * tiles : (j + 1) * tiles] = gathered[p][
                    match_ref[j * ring * near + to]
                ]
            partner_copy(p, r).start()
        selected[p][pl.ds(u * sources * tiles, tiles)] = gathered[p][clus]
        for j in range(sources - 1):
            selected[p][pl.ds((u * sources + 1 + j) * tiles, tiles)] = gathered[p][
                match_ref[j * ring * near + clus]
            ]

    def settle(p):
        for r in range(1, near):
            from_u = (u + near - r) % near
            arrived(
                selected[p].at[pl.ds(from_u * sources * tiles, tiles)], own_recv.at[p, r - 1]
            )
            arrived(
                selected[p].at[pl.ds((from_u * sources + 1) * tiles, (sources - 1) * tiles)],
                partner_recv.at[p, r - 1],
            )

    def masked_rows(parts, b):
        rows = []
        for n in range(chosen):
            tile = tile_ref[b * chosen + n]
            mask = masks[half_ref[b * chosen + n]]
            for part in parts:
                block = part[tile].reshape(ROWS // 16, 16, LANES)
                rows.append((block * mask[None]).reshape(ROWS, LANES))
        return jnp.concatenate(rows, axis=0)

    exponent_scale = 1.0 / (math.sqrt(HEAD_DIM) * math.log(2.0))

    def weigh(b, query):
        keys = masked_rows(selected[:PARTS], b)
        scores[...] = lax.dot_general(
            query, keys, (((1,), (1,)), ((), ())), preferred_element_type=jnp.float32
        )
        step = 16
        for i in range(BLOCK // step):
            s = scores[i * step : (i + 1) * step, :]
            top = jnp.max(s, axis=1, keepdims=True)
            power = jnp.exp2((s - top) * exponent_scale)
            total = jnp.sum(power, axis=1, keepdims=True)
            powers[b, i * step : (i + 1) * step, :] = (power * (1.0 / total)).astype(jnp.bfloat16)

    def weigh_pair(w, carry):
        pair = queries[w]
        low, high = pair[:, :HEAD_DIM], pair[:, HEAD_DIM:]
        weigh(2 * w, jnp.concatenate([low, low], axis=1))
        weigh(2 * w + 1, jnp.concatenate([high, high], axis=1))
        return carry

    done = [0]

    def weigh_some(count):
        stop = min(done[0] + count, heads)
        if stop > done[0]:
            lax.fori_loop(done[0], stop, weigh_pair, 0)
        done[0] = stop

    def mix(b):
        values = masked_rows(selected[PARTS:], b)
        both = jnp.dot(powers[b], values, preferred_element_type=jnp.float32)
        return both + jnp.concatenate([both[:, HEAD_DIM:], both[:, :HEAD_DIM]], axis=1)

    def mix_pair(w):
        low, high = mix(2 * w), mix(2 * w + 1)
        lanes = lax.broadcasted_iota(jnp.int32, (BLOCK, LANES), 1)
        mixed_out[w] = jnp.where(lanes < HEAD_DIM, low, high).astype(jnp.bfloat16)

    def mix_send(r, carry):
        w = (h + r) % heads
        mix_pair(w)
        copy(mixed_out.at[w], mixed_in.at[h], mixed_send, mixed_recv, clus, w).start()
        return carry

    for part in range(PARTS):
        first_start(part)
    pack(v_ref, put_rows(1))
    pack(q_ref, put_q)
    for p in range(PHASES):
        enter(p)
        if p < PARTS:
            first_start(PARTS + p)
        if p == PARTS - 1:
            q_start()
        if p > 0:
            forward(p - 1, far)
        if p == PHASES - 1:
            for part in range(PARTS):
                settle(part)
            arrived(queries, q_recv)
            weigh_some(4)
        for step in range(2, far):
            forward(p, step, functools.partial(weigh_some, 2 if p == PHASES - 1 else 0))
            if step == 2 and p > 0:
                leave(p - 1)
    forward(PHASES - 1, far, functools.partial(weigh_some, 2))
    leave(PHASES - 1)
    weigh_some(heads)
    for part in range(PARTS):
        settle(PARTS + part)

    lax.fori_loop(1, heads, mix_send, 0)
    mix_pair(h)
    pltpu.make_async_copy(mixed_out.at[h], mixed_in.at[h], mixed_recv).start()

    for p in range(PHASES):
        arrived(packed.at[p, 0 : heads - 1], first_send.at[p])

        @pl.when(jnp.logical_not(same))
        def _():
            first_copy_same(p).wait_send()

        for step in range(1, far + 1):
            for part in range(2):
                for way in range(2):
                    if step < far or part == way:
                        ring_copy(p, way, step, part).wait_send()
        for r in range(1, near):
            own_copy(p, r).wait_send()
            partner_copy(p, r).wait_send()
    arrived(packed_q.at[0 : heads - 1], q_send)
    arrived(mixed_out.at[0 : heads - 1], mixed_send)

    arrived(mixed_in, mixed_recv)
    step = 32
    for i in range(BLOCK // step):
        rows = slice(i * step, (i + 1) * step)
        firsts, seconds = [], []
        for t in range(heads // 2):
            even = mixed_in[2 * t, rows]
            odd = mixed_in[2 * t + 1, rows]
            firsts.append(jnp.concatenate([even[:, :HEAD_DIM], odd[:, :HEAD_DIM]], axis=1))
            seconds.append(jnp.concatenate([even[:, HEAD_DIM:], odd[:, HEAD_DIM:]], axis=1))
        for at, group in ((0, firsts), (BLOCK, seconds)):
            whole = jnp.concatenate(group, axis=1).astype(jnp.float32)
            mean_square = jnp.mean(whole * whole, axis=1, keepdims=True)
            normed = whole * lax.rsqrt(mean_square + 1e-06) * gain_ref[...]
            out_ref[at + i * step : at + (i + 1) * step, :] = normed.astype(out_ref.dtype)


def local(shape, node_queries, node_keys, node_values, matchings, patterns, out_gain):
    clusters, heads = shape
    near = NEAR if clusters >= 4 * NEAR else 2
    ring = clusters // near
    blocks, chosen = patterns.shape[1:]
    tiles = heads // near
    far = ring // 2
    width = node_queries.shape[1]
    pattern = patterns.reshape(-1)
    source = pattern // blocks
    pair = (pattern % blocks) // 2
    tile_at = ((pair % near) * 4 + source) * tiles + pair // near
    half = pattern % 2
    dtype = node_queries.dtype
    vmem = pl.BlockSpec(memory_space=pltpu.VMEM)
    smem = pl.BlockSpec(memory_space=pltpu.SMEM)
    dma = pltpu.SemaphoreType.DMA
    scratch = [
        pltpu.VMEM((PHASES, heads, ROWS, LANES), dtype),
        pltpu.VMEM((heads, BLOCK, LANES), dtype),
        pltpu.VMEM((PHASES, near - 1, 3 * tiles, ROWS, LANES), dtype),
        pltpu.VMEM((heads, BLOCK, LANES), dtype),
        pltpu.VMEM((blocks, BLOCK, chosen * BLOCK), dtype),
        pltpu.VMEM((BLOCK, chosen * BLOCK), jnp.float32),
        pltpu.VMEM((2, 16, LANES), dtype),
        pltpu.VMEM((heads, BLOCK, LANES), dtype),
        pltpu.VMEM((heads, BLOCK, LANES), dtype),
    ]
    scratch += [pltpu.VMEM((clusters, tiles, ROWS, LANES), dtype)] * PHASES
    scratch += [pltpu.VMEM((near * 4 * tiles, ROWS, LANES), dtype)] * PHASES
    scratch += [
        dma((PHASES,)),
        dma((PHASES,)),
        dma((PHASES,)),
        dma((PHASES, 2, far, 2)),
        dma((PHASES, 2, far, 2)),
        dma((PHASES, near - 1)),
        dma((PHASES, near - 1)),
        dma((PHASES, near - 1)),
        dma((PHASES, near - 1)),
        dma,
        dma,
        dma,
        dma,
    ]
    return pl.pallas_call(
        functools.partial(attention_kernel, (heads, ring, near, chosen)),
        out_shape=jax.ShapeDtypeStruct(node_queries.shape, dtype),
        in_specs=[smem] * 3 + [vmem] * 4,
        out_specs=vmem,
        scratch_shapes=scratch,
        compiler_params=pltpu.CompilerParams(
            collective_id=0, has_side_effects=True, vmem_limit_bytes=56 * 1024 * 1024
        ),
    )(
        tile_at,
        half,
        matchings.reshape(-1),
        node_queries,
        node_keys,
        node_values,
        out_gain.reshape(1, width),
    )


def solution(mesh):
    in_specs = (
        P(("clus", "head"), None),
        P(("clus", "head"), None),
        P(("clus", "head"), None),
        P(),
        P("clus", None, None),
        P(),
    )
    out_specs = P(("clus", "head"), None)
    return jax.shard_map(
        functools.partial(local, (mesh.shape["clus"], mesh.shape["head"])),
        mesh=mesh,
        in_specs=in_specs,
        out_specs=out_specs,
        check_vma=False,
    )
```

time: 384 us -> 141 us (0.37); the launches traced: 377 us -> 140 us
  Pallas kernels: 0 us -> 135 us
  waiting for transfers between devices: 134 us -> 0 us
  local copies, waits for them, and re-layouts: 129 us -> 4.08 us
  starting transfers between devices: 39.2 us -> 0 us
  matrix products: 34.1 us -> 0 us
  other arithmetic: 22.3 us -> 0.62 us
  blocking collectives: 17.7 us -> 0 us
    pallas_call x0 -> x1, Pallas kernels: none -> 135 us  [local(): pl.pallas_call(functools.partial(attention_kernel, (heads, ring, near, ch...]
    all_to_all x5 -> x0, waiting for transfers between devices: 134 us -> none  [the longest x1 67.7 us: local(): lax.all_to_all(chosen, 'clus', split_axis=1, concat_axis=3, tiled=True)]
    gather x17 -> x0, local copies, waits for them, and re-layouts: 39.3 us -> none  [the longest x8 18.3 us: one_group(): jnp.take(value_blocks, chosen, axis=0)]
    all_to_all x5 -> x0, starting transfers between devices: 39.2 us -> none  [the longest x1 13.4 us: local(): lax.all_to_all(node_keys, 'head', split_axis=1, concat_axis=0, tiled=True)]
    another operation x19 -> x0, local copies, waits for them, and re-layouts: 31.4 us -> none
    dot_general x8 -> x0, matrix products: 20.6 us -> none  [one_group(): jnp.einsum('bhqk,bkhd->bqhd', weights, value_group, preferred_element_typ...]
    select_n x10 -> x1, other arithmetic: 19.9 us -> 0.62 us  [local(): half = pattern % 2]
    all_to_all x1 -> x0, blocking collectives: 17.7 us -> none  [local(): lax.all_to_all(mixed_rows, 'head', split_axis=0, concat_axis=1, tiled=True)]
  transfers between devices with their start and end apart: 5 -> 0, of which waited for: 5 -> 0; matrix products, arithmetic and copies ran while one was open for 5% -> 0% of each run, Pallas kernels for 0% -> 0%
where the time goes in v1:
time: 141 us; the launch traced here: 140 us
  Pallas kernels  135 us (96%)
  local copies, waits for them, and re-layouts  4.08 us (3%)
    pallas_call x1, Pallas kernels, local(): pl.pallas_call(functools.partial(attention_kernel, (heads, ring, near, ch...  135 us

profile of v1, /device:TPU:1, one launch (start us, length us, event | category | flops | bytes accessed | tf_op | source)
XLA Modules:
  0.0 139.7 jit_solution(4739447112386079570)
XLA Ops:
  0.0 1.3 reshape.10.match_ref
  1.3 0.8 copy.7
  2.1 0.1 reshape.9
  2.2 0.6 add_select_fusion
  2.8 135.0 %shard_map.64 = bf16[256,1024]{1,0:T(8,128)(2,1)} custom-call(s32[384]{0:T(512)} %get-tuple-element.6.tile_ref, s32[384]{0:T(512)} %get-tuple-element.5.half_ref, s32[96]{0:T(128)} %reshape.10.match_ref, bf16[256,1024]{1,0:T(8,128)(2,1)} %q_ref.1, bf16[256,1024]{1,0:T(8,128)(2,1)} %k_ref.1, bf16[256,1024]{1,0:T(8,128)(2,1)} %v_ref.1, f32[1,1024]{1,0:T(1,128)} %bitcast.1), custom_call_target="tpu_custom_call" | custom-call | tf_op jit(solution)/shard_map/pallas_call | solution.py:446
  137.8 1.9 %copy.9 = bf16[256,1024]{1,0:T(8,128)(2,1)} copy(bf16[256,1024]{1,0:T(8,128)(2,1)} %shard_map.64) | data formatting | bytes 1048576

commit v2 on v1

v2 whole, which is shorter than its diff:
```python
import functools
import math

import jax
import jax.numpy as jnp
from jax import lax
from jax.experimental import pallas as pl
from jax.experimental.pallas import tpu as pltpu
from jax.sharding import PartitionSpec as P

HEAD_DIM = 64
BLOCK = 128
LANES = 128
PARTS = 4
ROWS = BLOCK // PARTS
PHASES = 2 * PARTS
SIDES = 2
SIDE = HEAD_DIM // SIDES
NEAR = 4
MESH = pl.DeviceIdType.MESH


def attention_kernel(
    dims,
    pattern_ref,
    match_ref,
    q_hbm,
    k_hbm,
    v_hbm,
    out_ref,
    q_ref,
    k_ref,
    v_ref,
    packed,
    packed_q,
    staged,
    queries,
    powers,
    scores,
    masks,
    mixed_out,
    mixed_in,
    ahead,
    tile_ref,
    half_ref,
    *rest,
):
    heads, ring, near, chosen, blocks = dims
    gathered = rest[:PHASES]
    selected = rest[PHASES : 2 * PHASES]
    (
        load,
        first_send,
        first_send_same,
        first_recv,
        ring_send,
        ring_recv,
        own_send,
        own_recv,
        partner_send,
        partner_recv,
        q_send,
        q_recv,
        mixed_send,
        mixed_recv,
    ) = rest[2 * PHASES :]
    tiles = heads // near
    sources = 4
    far = ring // 2
    clus = lax.axis_index("clus")
    h = lax.axis_index("head")
    y = clus // near
    u = clus % near
    home = h % near
    same = home == u

    def copy(src, dst, send, recv, to_clus, to_head):
        return pltpu.make_async_remote_copy(
            src_ref=src,
            dst_ref=dst,
            send_sem=send,
            recv_sem=recv,
            device_id={"clus": to_clus, "head": to_head},
            device_id_type=MESH,
        )

    def arrived(ref, sem):
        pltpu.make_async_copy(ref, ref, sem).wait()

    loads = [
        pltpu.make_async_copy(src, dst, load.at[i])
        for i, (src, dst) in enumerate(((k_hbm, k_ref), (v_hbm, v_ref), (q_hbm, q_ref)))
    ]
    for one in loads:
        one.start()

    barrier = pltpu.get_barrier_semaphore()

    def greet(to_clus, to_head):
        pl.semaphore_signal(
            barrier, inc=1, device_id={"clus": to_clus, "head": to_head}, device_id_type=MESH
        )

    def greet_first(i, carry):
        to_clus = y * near + i // tiles
        to_head = u + near * (i % tiles)

        @pl.when(jnp.logical_or(to_clus != clus, to_head != h))
        def _():
            greet(to_clus, to_head)

        return carry

    def greet_head(r, carry):
        greet(clus, (h + r) % heads)
        return carry

    lax.fori_loop(0, near * tiles, greet_first, 0)
    lax.fori_loop(1, heads, greet_head, 0)
    for r in range(1, near):
        greet(y * near + (u + r) % near, h)
    above = ((y + 1) % ring) * near + u
    below = ((y + ring - 1) % ring) * near + u
    greet(above, h)
    greet(below, h)

    def pack(ref, put):
        for t in range(heads // 2):
            first = ref[0:BLOCK, t * LANES : (t + 1) * LANES]
            second = ref[BLOCK : 2 * BLOCK, t * LANES : (t + 1) * LANES]
            put(
                2 * t,
                jnp.concatenate([first[:, :HEAD_DIM], second[:, :HEAD_DIM]], axis=1),
            )
            put(
                2 * t + 1,
                jnp.concatenate([first[:, HEAD_DIM:], second[:, HEAD_DIM:]], axis=1),
            )

    def put_keys(head, tile):
        for part in range(PARTS):
            packed[part, head] = tile[part * ROWS : (part + 1) * ROWS]

    def put_values(head, tile):
        middle = BLOCK // 2
        for side in range(SIDES):
            pieces = [
                tile[rows, at + side * SIDE : at + (side + 1) * SIDE]
                for at in (0, HEAD_DIM)
                for rows in (slice(0, middle), slice(middle, BLOCK))
            ]
            wide = jnp.concatenate(pieces, axis=1)
            for part in range(2):
                packed[PARTS + 2 * side + part, head] = wide[part * ROWS : (part + 1) * ROWS]

    def put_q(head, tile):
        packed_q[head] = tile

    loads[0].wait()
    pack(k_ref, put_keys)
    lane = lax.broadcasted_iota(jnp.int32, (16, LANES), 1)
    for i in range(2):
        masks[i] = jnp.where(lane // HEAD_DIM == i, 1.0, 0.0).astype(masks.dtype)
    for i in range(4):
        masks[2 + i] = jnp.where(lane // SIDE == i, 1.0, 0.0).astype(masks.dtype)

    itself = jnp.where(same, 1, 0)
    pl.semaphore_wait(barrier, (near * tiles - itself) + (heads - 1) + (near - 1) + 2)

    def first_copy(p, r):
        g = (h + r) % heads
        return copy(
            packed.at[p, g],
            gathered[p].at[clus, h // near],
            first_send.at[p],
            first_recv.at[p],
            y * near + home,
            g,
        )

    def first_copy_same(p):
        return copy(
            packed.at[p, h],
            gathered[p].at[clus, h // near],
            first_send_same.at[p],
            first_recv.at[p],
            y * near + home,
            h,
        )

    def first_start(p):
        @pl.when(same)
        def _():
            pltpu.make_async_copy(
                packed.at[p, h], gathered[p].at[clus, h // near], first_recv.at[p]
            ).start()

        @pl.when(jnp.logical_not(same))
        def _():
            first_copy_same(p).start()

        def step(r, carry):
            first_copy(p, r).start()
            return carry

        lax.fori_loop(1, heads, step, 0)

    def q_start():
        pltpu.make_async_copy(packed_q.at[h], queries.at[h], q_recv).start()

        def step(r, carry):
            g = (h + r) % heads
            copy(packed_q.at[g], queries.at[h], q_send, q_recv, clus, g).start()
            return carry

        lax.fori_loop(1, heads, step, 0)

    def ring_cuts(p, way, step):
        if step == far:
            return (way,)
        if p == PHASES - 1 and step > 1:
            return (way, 1 - way)
        return (None,)

    def ring_ref(p, way, distance, cut):
        slot = (y + ring - distance) % ring if way == 0 else (y + distance) % ring
        if cut is None:
            return gathered[p].at[pl.ds(slot * near, near)]
        return gathered[p].at[pl.ds(slot * near + cut * (near // 2), near // 2)]

    def ring_copy(p, way, step, cut):
        ref = ring_ref(p, way, step - 1, cut)
        return copy(
            ref,
            ref,
            ring_send.at[p, way, step - 1, cut or 0],
            ring_recv.at[p, way, step - 1, cut or 0],
            above if way == 0 else below,
            h,
        )

    def ring_wait(p, way, step, cut):
        arrived(ring_ref(p, way, step, cut), ring_recv.at[p, way, step - 1, cut or 0])

    def own_copy(p, r):
        to = y * near + (u + r) % near
        return copy(
            gathered[p].at[to],
            selected[p].at[pl.ds(u * sources * tiles, tiles)],
            own_send.at[p, r - 1],
            own_recv.at[p, r - 1],
            to,
            h,
        )

    def partner_copy(p, r):
        return copy(
            staged.at[p, r - 1],
            selected[p].at[pl.ds((u * sources + 1) * tiles, (sources - 1) * tiles)],
            partner_send.at[p, r - 1],
            partner_recv.at[p, r - 1],
            y * near + (u + r) % near,
            h,
        )

    def enter(p):
        arrived(gathered[p].at[pl.ds(y * near, near)], first_recv.at[p])
        for way in range(2):
            ring_copy(p, way, 1, None).start()
        for r in range(1, near):
            own_copy(p, r).start()

    def forward(p, step, turn=None):
        for way in range(2):
            came = ring_cuts(p, way, step - 1)
            for i, cut in enumerate(ring_cuts(p, way, step)):
                if turn is None or turn == i:
                    if len(came) > 1:
                        ring_wait(p, way, step - 1, cut)
                    elif i == 0:
                        ring_wait(p, way, step - 1, None)
                    ring_copy(p, way, step, cut).start()

    def leave(p):
        for way in range(2):
            for cut in ring_cuts(p, way, far - 1)[1:]:
                ring_wait(p, way, far - 1, cut)
            ring_wait(p, way, far, way)
        for r in range(1, near):
            to = y * near + (u + r) % near
            for j in range(sources - 1):
                staged[p, r - 1, j * tiles : (j + 1) * tiles] = gathered[p][match_ref[j, to]]
            partner_copy(p, r).start()
        selected[p][pl.ds(u * sources * tiles, tiles)] = gathered[p][clus]
        for j in range(sources - 1):
            selected[p][pl.ds((u * sources + 1 + j) * tiles, tiles)] = gathered[p][
                match_ref[j, clus]
            ]

    def settle(p):
        for r in range(1, near):
            from_u = (u + near - r) % near
            arrived(
                selected[p].at[pl.ds(from_u * sources * tiles, tiles)], own_recv.at[p, r - 1]
            )
            arrived(
                selected[p].at[pl.ds((from_u * sources + 1) * tiles, (sources - 1) * tiles)],
                partner_recv.at[p, r - 1],
            )

    block_bits, near_bits = (count.bit_length() - 1 for count in (blocks, near))

    def note_blocks(b, carry):
        for n in range(chosen):
            block = pattern_ref[n, 0, b]
            source = block >> block_bits
            pair = (block & (blocks - 1)) >> 1
            tile = ((pair & (near - 1)) * sources + source) * tiles + (pair >> near_bits)
            tile_ref[b * chosen + n] = tile
            half_ref[b * chosen + n] = block & 1
        return carry

    def find(b, n):
        return tile_ref[b * chosen + n], half_ref[b * chosen + n]

    def masked(part, tile, mask):
        block = part[tile].reshape(ROWS // 16, 16, LANES)
        return (block * mask[None]).reshape(ROWS, LANES)

    def key_rows(b):
        rows = []
        for part in range(2):
            for n in range(chosen):
                tile, half = find(b, n)
                mask = masks[half]
                rows += [masked(selected[2 * i + part], tile, mask) for i in range(2)]
        return jnp.concatenate(rows, axis=0)

    def value_rows(b, side, parts):
        rows = []
        for part in parts:
            for n in range(chosen):
                tile, half = find(b, n)
                for i in range(2):
                    mask = masks[2 + 2 * half + i]
                    rows.append(masked(selected[PARTS + 2 * side + part], tile, mask))
        return jnp.concatenate(rows, axis=0)

    exponent_scale = 1.0 / (math.sqrt(HEAD_DIM) * math.log(2.0))

    def weigh(b, query, slot):
        keys = key_rows(b)
        scores[slot] = lax.dot_general(
            query, keys, (((1,), (1,)), ((), ())), preferred_element_type=jnp.float32
        )
        step = 16
        for i in range(BLOCK // step):
            s = scores[slot, i * step : (i + 1) * step, :]
            top = jnp.max(s, axis=1, keepdims=True)
            power = jnp.exp2((s - top) * exponent_scale)
            total = jnp.sum(power, axis=1, keepdims=True)
            powers[b, i * step : (i + 1) * step, :] = (power * (1.0 / total)).astype(jnp.bfloat16)

    def weigh_pair(w, carry):
        pair = queries[w]
        low, high = pair[:, :HEAD_DIM], pair[:, HEAD_DIM:]
        weigh(2 * w, jnp.concatenate([low, low], axis=1), 0)
        weigh(2 * w + 1, jnp.concatenate([high, high], axis=1), 1)
        return carry

    done = [0]

    def weigh_some(count):
        stop = min(done[0] + count, heads)
        if stop > done[0]:
            lax.fori_loop(done[0], stop, weigh_pair, 0)
        done[0] = stop

    def product(b, side, parts):
        width = chosen * BLOCK // 2
        columns = slice(parts[0] * width, (parts[-1] + 1) * width)
        return jnp.dot(
            powers[b, :, columns],
            value_rows(b, side, parts),
            preferred_element_type=jnp.float32,
        )

    def mix_ahead(i, carry):
        found = [product(4 * i + j, SIDES - 1, (0,)) for j in range(4)]
        for j in range(4):
            ahead[4 * i + j] = found[j]
        return carry

    def mix(b, side):
        if side < SIDES - 1:
            spread = product(b, side, (0, 1))
        else:
            spread = ahead[b] + product(b, side, (1,))
        spread = spread + pltpu.roll(spread, 2 * SIDE, 1)
        return spread + pltpu.roll(spread, SIDE, 1)

    def mix_pair(w, side):
        low, high = mix(2 * w, side), mix(2 * w + 1, side)
        middle = BLOCK // 2
        group = lax.broadcasted_iota(jnp.int32, (middle, LANES), 1) // SIDE
        tile = jnp.where(
            group < 2,
            jnp.where(group == 0, low[:middle], low[middle:]),
            jnp.where(group == 2, high[:middle], high[middle:]),
        )
        return tile.astype(jnp.bfloat16)

    def mix_send(w, side):
        copy(
            mixed_out.at[side, w],
            mixed_in.at[side, h],
            mixed_send.at[side],
            mixed_recv.at[side],
            clus,
            w,
        ).start()

    def mix_two(side, i, carry):
        pairs = [(h + 2 * i + j) % heads for j in (1, 2)]
        found = [mix_pair(w, side) for w in pairs]
        for w, tile in zip(pairs, found):
            mixed_out[side, w] = tile
        for w in pairs:
            mix_send(w, side)
        return carry

    mixed = [0] * SIDES

    def mix_some(side, count):
        end = heads // 2
        stop = min(mixed[side] + count, end - 1)
        if stop > mixed[side]:
            lax.fori_loop(mixed[side], stop, functools.partial(mix_two, side), 0)
        mixed[side] = stop
        if count >= end:
            other = (h + heads - 1) % heads
            found = mix_pair(other, side), mix_pair(h, side)
            mixed_out[side, other] = found[0]
            mixed_out[side, h] = found[1]
            mix_send(other, side)
            pltpu.make_async_copy(
                mixed_out.at[side, h], mixed_in.at[side, h], mixed_recv.at[side]
            ).start()

    first_start(0)
    first_start(1)
    enter(0)
    first_start(2)
    enter(1)
    first_start(3)
    loads[1].wait()
    pack(v_ref, put_values)
    forward(0, 2)
    loads[2].wait()
    pack(q_ref, put_q)
    forward(1, 2)
    first_start(4)
    forward(0, 3)
    enter(2)
    first_start(5)
    forward(0, 4)
    forward(1, 3)
    leave(0)
    forward(2, 2)
    first_start(6)
    lax.fori_loop(0, blocks, note_blocks, 0)
    forward(1, 4)
    for p in range(3, PHASES):
        enter(p)
        if p == 3:
            first_start(7)
        if p == 4:
            q_start()
        if p == PHASES - 1:
            weigh_some(2)
        forward(p - 1, 3)
        leave(p - 2)
        if p == PHASES - 2:
            for part in range(PARTS):
                settle(part)
            arrived(queries, q_recv)
        if p >= PHASES - 2:
            weigh_some(3)
        forward(p, 2)
        if p >= PHASES - 2:
            weigh_some(3)
        forward(p - 1, 4)
        if p == PHASES - 2:
            weigh_some(2)
    last = PHASES - 1
    weigh_some(heads)
    settle(PARTS)
    settle(PARTS + 1)
    mix_some(0, 1)
    forward(last, 3, 0)
    mix_some(0, 1)
    forward(last, 3, 1)
    mix_some(0, 1)
    leave(last - 1)
    mix_some(0, 1)
    forward(last, 4)
    mix_some(0, 2)
    leave(last)
    mix_some(0, heads)
    settle(last - 1)
    lax.fori_loop(0, heads // 2, mix_ahead, 0)
    settle(last)
    mix_some(1, heads)

    for p in range(PHASES):
        arrived(packed.at[p, 0 : heads - 1], first_send.at[p])

        @pl.when(jnp.logical_not(same))
        def _():
            first_copy_same(p).wait_send()

        for step in range(1, far + 1):
            for way in range(2):
                for cut in ring_cuts(p, way, step):
                    ring_copy(p, way, step, cut).wait_send()
        for r in range(1, near):
            own_copy(p, r).wait_send()
            partner_copy(p, r).wait_send()
    arrived(packed_q.at[0 : heads - 1], q_send)
    for side in range(SIDES):
        arrived(mixed_out.at[side, 0 : heads - 1], mixed_send.at[side])
        arrived(mixed_in.at[side], mixed_recv.at[side])

    step = 16
    for group in range(4):
        lanes = slice(group * SIDE, (group + 1) * SIDE)
        for i in range(BLOCK // 2 // step):
            rows = slice(i * step, (i + 1) * step)
            pieces = [
                mixed_in[side, head, rows][:, lanes]
                for head in range(heads)
                for side in range(SIDES)
            ]
            normed = jnp.concatenate(pieces, axis=1)
            at = group * (BLOCK // 2) + i * step
            out_ref[at : at + step, :] = normed.astype(out_ref.dtype)


def local(shape, node_queries, node_keys, node_values, matchings, patterns, out_gain):
    clusters, heads = shape
    near = NEAR if clusters % (8 * NEAR) == 0 else 2
    ring = clusters // near
    blocks, chosen = patterns.shape[1:]
    tiles = heads // near
    far = ring // 2
    width = node_queries.shape[1]
    dtype = node_queries.dtype
    vmem = pl.BlockSpec(memory_space=pltpu.VMEM)
    smem = pl.BlockSpec(memory_space=pltpu.SMEM)
    dma = pltpu.SemaphoreType.DMA
    scratch = [
        pltpu.VMEM(node_queries.shape, dtype),
        pltpu.VMEM(node_queries.shape, dtype),
        pltpu.VMEM(node_queries.shape, dtype),
        pltpu.VMEM((PHASES, heads, ROWS, LANES), dtype),
        pltpu.VMEM((heads, BLOCK, LANES), dtype),
        pltpu.VMEM((PHASES, near - 1, 3 * tiles, ROWS, LANES), dtype),
        pltpu.VMEM((heads, BLOCK, LANES), dtype),
        pltpu.VMEM((blocks, BLOCK, chosen * BLOCK), dtype),
        pltpu.VMEM((2, BLOCK, chosen * BLOCK), jnp.float32),
        pltpu.VMEM((6, 16, LANES), dtype),
        pltpu.VMEM((SIDES, heads, BLOCK // SIDES, LANES), dtype),
        pltpu.VMEM((SIDES, heads, BLOCK // SIDES, LANES), dtype),
        pltpu.VMEM((blocks, BLOCK, LANES), jnp.float32),
        pltpu.SMEM((blocks * chosen,), jnp.int32),
        pltpu.SMEM((blocks * chosen,), jnp.int32),
    ]
    scratch += [pltpu.VMEM((clusters, tiles, ROWS, LANES), dtype)] * PHASES
    scratch += [pltpu.VMEM((near * 4 * tiles, ROWS, LANES), dtype)] * PHASES
    scratch += [
        dma((3,)),
        dma((PHASES,)),
        dma((PHASES,)),
        dma((PHASES,)),
        dma((PHASES, 2, far, 2)),
        dma((PHASES, 2, far, 2)),
        dma((PHASES, near - 1)),
        dma((PHASES, near - 1)),
        dma((PHASES, near - 1)),
        dma((PHASES, near - 1)),
        dma,
        dma,
        dma((SIDES,)),
        dma((SIDES,)),
    ]
    rows = pl.pallas_call(
        functools.partial(attention_kernel, (heads, ring, near, chosen, blocks)),
        out_shape=jax.ShapeDtypeStruct(node_queries.shape, dtype),
        in_specs=[smem] * 2 + [pl.BlockSpec(memory_space=pl.ANY)] * 3,
        out_specs=vmem,
        scratch_shapes=scratch,
        compiler_params=pltpu.CompilerParams(
            collective_id=0, has_side_effects=True, vmem_limit_bytes=56 * 1024 * 1024
        ),
    )(
        jnp.transpose(patterns, (2, 0, 1)),
        matchings,
        node_queries,
        node_keys,
        node_values,
    ).astype(jnp.float32)
    mean_square = jnp.mean(rows * rows, axis=-1, keepdims=True)
    return (rows * lax.rsqrt(mean_square + 1e-06) * out_gain).astype(jnp.bfloat16)


def solution(mesh):
    in_specs = (
        P(("clus", "head"), None),
        P(("clus", "head"), None),
        P(("clus", "head"), None),
        P(),
        P("clus", None, None),
        P(),
    )
    out_specs = P(("clus", "head"), None)
    return jax.shard_map(
        functools.partial(local, (mesh.shape["clus"], mesh.shape["head"])),
        mesh=mesh,
        in_specs=in_specs,
        out_specs=out_specs,
        check_vma=False,
    )
```

time: 141 us -> 131 us (0.929)
  Pallas kernels: 135 us -> 128 us
  local copies, waits for them, and re-layouts: 4.08 us -> 0.01 us
  other arithmetic: 0.62 us -> 2.28 us
    pallas_call x1, Pallas kernels: 135 us -> 128 us  [local(): pl.pallas_call(functools.partial(attention_kernel, (heads, ring, near, ch...]
    unnamed x2 -> x4, local copies, waits for them, and re-layouts: 2.64 us -> 0.01 us
    reshape x2 -> x0, local copies, waits for them, and re-layouts: 1.44 us -> none  [the longest x1 1.34 us: local(): matchings.reshape(-1)]
where the time goes in v2:
time: 131 us
  Pallas kernels  128 us (98%)
  other arithmetic  2.28 us (2%)
    pallas_call x1, Pallas kernels, local(): pl.pallas_call(functools.partial(attention_kernel, (heads, ring, near, ch...  128 us

profile of v2, /device:TPU:1, one launch (start us, length us, event | category | flops | bytes accessed | tf_op | source)
XLA Modules:
  0.0 130.6 jit_solution(5024848571870439355)
XLA Ops:
  0.0 0.0 copy-start.1
  0.0 128.3 %shard_map.64 = bf16[256,1024]{1,0:T(8,128)(2,1)} custom-call(s32[12,1,32]{2,1,0:T(1,128)} %bitcast.1, s32[3,32]{1,0:T(4,128)} %match_ref.1, bf16[256,1024]{1,0:T(8,128)(2,1)} %q_hbm.1, bf16[256,1024]{1,0:T(8,128)(2,1)} %k_hbm.1, bf16[256,1024]{1,0:T(8,128)(2,1)} %v_hbm.1), custom_call_target="tpu_custom_call" | custom-call | tf_op jit(solution)/shard_map/pallas_call | solution.py:596
  128.3 0.0 copy-start
  128.3 1.3 fusion
  129.6 0.0 copy-done.1
  129.6 0.0 copy-done
  129.6 1.0 fusion.2
  (1 shorter events, 0.0 us)
Async XLA Ops:
  0.0 129.6 %copy-start.1 = (f32[1024]{0:T(1024)S(1)}, f32[1024]{0:T(1024)}, u32[]{:S(2)}) copy-start(f32[1024]{0:T(1024)} %param.11) | copy-start | bytes 12292
  128.3 1.3 %copy-start = (bf16[256,1024]{1,0:T(8,128)(2,1)S(1)}, bf16[256,1024]{1,0:T(8,128)(2,1)}, u32[]{:S(2)}) copy-start(bf16[256,1024]{1,0:T(8,128)(2,1)} %shard_map.64) | copy-start | bytes 1572868

commit v3 on v2

--- a/solution.py
+++ b/solution.py
@@ -84,6 +84,9 @@
             device_id_type=MESH,
         )
 
+    def far_first(r):
+        return (h + heads // 2 + (r // 2) * (2 * (r % 2) - 1)) % heads
+
     def arrived(ref, sem):
         pltpu.make_async_copy(ref, ref, sem).wait()
 
@@ -168,7 +171,7 @@
     pl.semaphore_wait(barrier, (near * tiles - itself) + (heads - 1) + (near - 1) + 2)
 
     def first_copy(p, r):
-        g = (h + r) % heads
+        g = far_first(r)
         return copy(
             packed.at[p, g],
             gathered[p].at[clus, h // near],
@@ -209,7 +212,7 @@
         pltpu.make_async_copy(packed_q.at[h], queries.at[h], q_recv).start()
 
         def step(r, carry):
-            g = (h + r) % heads
+            g = far_first(r)
             copy(packed_q.at[g], queries.at[h], q_send, q_recv, clus, g).start()
             return carry
 
@@ -421,7 +424,7 @@
         ).start()
 
     def mix_two(side, i, carry):
-        pairs = [(h + 2 * i + j) % heads for j in (1, 2)]
+        pairs = [far_first(2 * i + j) for j in (1, 2)]
         found = [mix_pair(w, side) for w in pairs]
         for w, tile in zip(pairs, found):
             mixed_out[side, w] = tile
@@ -438,7 +441,7 @@
             lax.fori_loop(mixed[side], stop, functools.partial(mix_two, side), 0)
         mixed[side] = stop
         if count >= end:
-            other = (h + heads - 1) % heads
+            other = far_first(heads - 1)
             found = mix_pair(other, side), mix_pair(h, side)
             mixed_out[side, other] = found[0]
             mixed_out[side, h] = found[1]
@@ -546,6 +549,15 @@
             out_ref[at : at + step, :] = normed.astype(out_ref.dtype)
 
 
+def norm_kernel(rows_ref, gain_ref, out_ref):
+    step = 32
+    for at in range(0, rows_ref.shape[0], step):
+        rows = rows_ref[at : at + step, :].astype(jnp.float32)
+        mean_square = jnp.mean(rows * rows, axis=1, keepdims=True)
+        normed = rows * lax.rsqrt(mean_square + 1e-06) * gain_ref[...]
+        out_ref[at : at + step, :] = normed.astype(out_ref.dtype)
+
+
 def local(shape, node_queries, node_keys, node_values, matchings, patterns, out_gain):
     clusters, heads = shape
     near = NEAR if clusters % (8 * NEAR) == 0 else 2
@@ -608,9 +620,13 @@
         node_queries,
         node_keys,
         node_values,
-    ).astype(jnp.float32)
-    mean_square = jnp.mean(rows * rows, axis=-1, keepdims=True)
-    return (rows * lax.rsqrt(mean_square + 1e-06) * out_gain).astype(jnp.bfloat16)
+    )
+    return pl.pallas_call(
+        norm_kernel,
+        out_shape=jax.ShapeDtypeStruct(rows.shape, dtype),
+        in_specs=[vmem, vmem],
+        out_specs=vmem,
+    )(rows, out_gain.reshape(1, width))
 
 
 def solution(mesh):

time: 131 us -> 130 us (level)
  other arithmetic: 2.28 us -> 0 us
  Pallas kernels: 128 us -> 130 us
    pallas_call x0 -> x1, Pallas kernels: none -> 2.05 us  [local(): pl.pallas_call(norm_kernel, out_shape=jax.ShapeDtypeStruct(rows.shape, dt...]
where the time goes in v3:
time: 130 us
  Pallas kernels  130 us (100%)
    pallas_call x1, Pallas kernels, local(): pl.pallas_call(functools.partial(attention_kernel, (heads, ring, near, ch...  128 us

profile of v3, /device:TPU:1, one launch (start us, length us, event | category | flops | bytes accessed | tf_op | source)
XLA Modules:
  0.0 129.7 jit_solution(9958857665850082795)
XLA Ops:
  0.0 127.6 %shard_map.64.rows_ref = bf16[256,1024]{1,0:T(8,128)(2,1)} custom-call(s32[12,1,32]{2,1,0:T(1,128)} %bitcast.2, s32[3,32]{1,0:T(4,128)} %match_ref.1, bf16[256,1024]{1,0:T(8,128)(2,1)} %q_hbm.1, bf16[256,1024]{1,0:T(8,128)(2,1)} %k_hbm.1, bf16[256,1024]{1,0:T(8,128)(2,1)} %v_hbm.1), custom_call_target="tpu_custom_call" | custom-call | tf_op jit(solution)/shard_map/pallas_call | solution.py:608
  127.6 2.1 %shard_map.65 = bf16[256,1024]{1,0:T(8,128)(2,1)} custom-call(bf16[256,1024]{1,0:T(8,128)(2,1)} %shard_map.64.rows_ref, f32[1,1024]{1,0:T(1,128)} %bitcast.3), custom_call_target="tpu_custom_call" | custom-call | tf_op jit(solution)/shard_map/pallas_call | solution.py:624

commit v4 on v3

--- a/solution.py
+++ b/solution.py
@@ -424,7 +424,7 @@
         ).start()
 
     def mix_two(side, i, carry):
-        pairs = [far_first(2 * i + j) for j in (1, 2)]
+        pairs = [far_first(2 * i + j) for j in (2, 3)]
         found = [mix_pair(w, side) for w in pairs]
         for w, tile in zip(pairs, found):
             mixed_out[side, w] = tile
@@ -436,16 +436,16 @@
 
     def mix_some(side, count):
         end = heads // 2
+        if mixed[side] == 0:
+            first = far_first(1)
+            mixed_out[side, first] = mix_pair(first, side)
+            mix_send(first, side)
         stop = min(mixed[side] + count, end - 1)
         if stop > mixed[side]:
             lax.fori_loop(mixed[side], stop, functools.partial(mix_two, side), 0)
         mixed[side] = stop
         if count >= end:
-            other = far_first(heads - 1)
-            found = mix_pair(other, side), mix_pair(h, side)
-            mixed_out[side, other] = found[0]
-            mixed_out[side, h] = found[1]
-            mix_send(other, side)
+            mixed_out[side, h] = mix_pair(h, side)
             pltpu.make_async_copy(
                 mixed_out.at[side, h], mixed_in.at[side, h], mixed_recv.at[side]
             ).start()

time: 130 us -> 130 us (level)
  no operation moved by 1% of the time
where the time goes in v4:
time: 130 us
  Pallas kernels  130 us (100%)
    pallas_call x1, Pallas kernels, local(): pl.pallas_call(functools.partial(attention_kernel, (heads, ring, near, ch...  128 us

profile of v4, /device:TPU:1, one launch (start us, length us, event | category | flops | bytes accessed | tf_op | source)
XLA Modules:
  0.0 130.0 jit_solution(5921543245160535988)
XLA Ops:
  0.0 127.9 %shard_map.64.rows_ref = bf16[256,1024]{1,0:T(8,128)(2,1)} custom-call(s32[12,1,32]{2,1,0:T(1,128)} %bitcast.2, s32[3,32]{1,0:T(4,128)} %match_ref.1, bf16[256,1024]{1,0:T(8,128)(2,1)} %q_hbm.1, bf16[256,1024]{1,0:T(8,128)(2,1)} %k_hbm.1, bf16[256,1024]{1,0:T(8,128)(2,1)} %v_hbm.1), custom_call_target="tpu_custom_call" | custom-call | tf_op jit(solution)/shard_map/pallas_call | solution.py:608
  128.0 2.1 %shard_map.65 = bf16[256,1024]{1,0:T(8,128)(2,1)} custom-call(bf16[256,1024]{1,0:T(8,128)(2,1)} %shard_map.64.rows_ref, f32[1,1024]{1,0:T(1,128)} %bitcast.3), custom_call_target="tpu_custom_call" | custom-call | tf_op jit(solution)/shard_map/pallas_call | solution.py:624
